TPU v7x, 256 devices: a whole 4x4x8 slice. The times are simulated.
256 devices in a mesh: region: 256 (over y, x, z, core).
Axes of the slice: x: 4, y: 4, z: 8, core: 2. Of those that a mesh axis runs over, the one named last changes fastest.
Arguments:
- pixels: bfloat16 [1024, 512, 2, 256], P('region'), may hold values from -6 to 6
- leaf_valid: int32 [1024, 512], P('region'), may hold values 0 or 1
- leaf_basis: bfloat16 [256, 32], replicated, may hold values from -0.75 to 0.75
- near_blocks: bfloat16 [9, 256, 256], replicated, may hold values from -0.125 to 0.125
- transfer: float32 [2, 32, 32], replicated, may hold values from -1 to 1
- leaf_coupling: float32 [40, 32, 32], replicated, may hold values from -0.078125 to 0.078125
- top_coupling: float32 [160, 32, 32], replicated, may hold values from -0.001953125 to 0.001953125
- top_partner: int32 [480, 8], replicated, may hold values from 0 to 479, as said below
- top_offset: int32 [480, 8], replicated, may hold values from 0 to 159
- top_count: int32 [480], replicated, may hold values from 1 to 8
Outputs:
- covariance_product: float32 [1024, 512, 2, 256], P('region')
Inputs may be any that keep to these rules, and one draw needn't show every extreme that they name: `top_partner`: rows 0 to 256 - 1 are the band nodes, then each level above takes half as many rows; every entry names a node of its row's own level, two or more places away from the row's node in that level's cyclic order.
All inputs are finite; a program needn't handle non-finite values. No bound on the sum of `leaf_valid` on one device may be relied on, other than what follows from the above.
Results may differ from a plain program's by a relative error of at most 0.0003.
Values may be sent and summed in bfloat16 or wider, within the bound.
A program may use at most 256 MiB of HBM per device.

v0:
```python
import functools

import jax
import jax.numpy as jnp
from jax import lax
from jax.experimental import pallas as pl
from jax.experimental.pallas import tpu as pltpu
from jax.sharding import PartitionSpec as P

MESH = pl.DeviceIdType.MESH
F32 = jnp.float32
BF16 = jnp.bfloat16
NN = (((1,), (0,)), ((), ()))
NT = (((1,), (1,)), ((), ()))
IN_ORDER = (1, 2, 0, 3)
VMEM_LIMIT = 56 << 20


def dot(a, b, dims=NN):
    return lax.dot_general(a, b, dims, preferred_element_type=F32)


def split(x):
    hi = x.astype(BF16)
    return hi, (x - hi.astype(F32)).astype(BF16)


def dot3(a, b, dims=NN):
    a_hi, a_lo = split(a)
    b_hi, b_lo = split(b)
    return dot(a_hi, b_hi, dims) + (dot(a_lo, b_hi, dims) + dot(a_hi, b_lo, dims))


def iota(shape, axis):
    return lax.broadcasted_iota(jnp.int32, shape, axis)


def tree_paths(transfer):
    side0, side1 = transfer[0], transfer[1]
    both = jnp.concatenate([side0, side1], 0)
    lanes = jnp.concatenate([side0, side1], 1)
    pairs = dot3(both, lanes)
    two = jnp.concatenate([pairs[:, :32], pairs[:, 32:]], 0)
    three = dot3(two, lanes)
    three = jnp.concatenate([three[:, :32], three[:, 32:]], 0)
    two_lanes = jnp.concatenate([two[32 * s : 32 * s + 32] for s in range(4)], 1)
    four = dot3(two, two_lanes)
    four = jnp.concatenate([four[:, 32 * s : 32 * s + 32] for s in range(4)], 0)
    return both, two, three, four


def mask_rows(valid):
    values = valid.astype(F32).astype(BF16)
    values = jnp.concatenate([values, values], 0)
    lane = iota((512, 1024), 1)
    leaf = (lane & 510) + (lane >> 9)
    pick = (iota((512, 1024), 0) == leaf).astype(F32).astype(BF16)
    return dot(values, pick)


def column(row):
    return jnp.concatenate(
        [jnp.broadcast_to(row[:, 128 * b : 128 * b + 128], (128, 128)).T for b in range(4)], 0
    )


def climb(packed, v_ref, w_ref, paths):
    _, _, three, four = paths
    merge = jnp.concatenate(
        [three[(c * 4 + i) * 32 : (c * 4 + i) * 32 + 32] for i in IN_ORDER for c in range(2)], 0
    )
    v_ref[:, 0:32] = dot3(packed, merge)
    rows = []
    for rhs in range(2):
        rows.append(
            jnp.concatenate(
                [v_ref[pl.ds(2 * b + rhs, 16, stride=32), :][:, 0:32] for b in range(16)], 1
            )
        )
    w_ref[:, 0:32] = dot3(jnp.concatenate(rows, 0), four)
    last = jnp.concatenate([w_ref[pl.ds(a, 2, stride=16), :][:, 0:32] for a in range(16)], 1)
    return dot3(jnp.concatenate([last, last, last, last], 0), four)[0:2]


def kernel_up(x, valid, bt, transfer, xm, mcol, packed, region, xs, basis, v_ref, w_ref, sem):
    copies = []
    for i in range(4):
        for c in range(2):
            for lt in range(2):
                copy = pltpu.make_async_copy(
                    x.at[i, :, c, :, pl.ds(lt * 128, 128)], xs.at[i, c, lt], sem.at[i, c, lt]
                )
                copy.start()
                copies.append(copy)
    basis[...] = jnp.zeros_like(basis)
    for at, i in enumerate(IN_ORDER):
        for c in range(2):
            basis[pl.ds(at * 64 + c * 32, 32), pl.ds((i * 2 + c) * 256, 256)] = bt[...]
    paths = tree_paths(transfer)
    rows = mask_rows(valid[...])
    for i in range(4):
        for c in range(2):
            col = column(rows[i : i + 1, c * 512 : c * 512 + 512]).astype(BF16)
            mcol[i, c] = col
            for lt in range(2):
                copies[(i * 2 + c) * 2 + lt].wait()
                part = xs.at[i, c, lt].reshape(512, 128)[...]
                xm[i, c, :, lt * 128 : lt * 128 + 128] = part * col
    pixels = jnp.concatenate([xm[i, c] for i in range(4) for c in range(2)], 1)
    packed[...] = dot(pixels, basis[...], NT)
    top = climb(packed[...], v_ref, w_ref, paths)
    region[0] = jnp.concatenate([top[0:1], top[1:2], jnp.zeros((1, 64), F32)], 1)


def kernel_move(n, xm, packed, region, hx, hc, table, px_s, px_r, cf_s, cf_r, g1_s, g1_r, g2_s, g2_r, own):
    me = lax.axis_index("region")
    right, left = lax.rem(me + 1, n), lax.rem(me + n - 1, n)
    group = me // 16
    spot = lax.rem(me, 16)
    groups = n // 16
    barrier = pltpu.get_barrier_semaphore()
    peers1 = [group * 16 + lax.rem(spot + k, 16) for k in range(1, 16)]
    peers2 = [lax.rem(group + k, groups) * 16 + spot for k in range(1, groups)]
    for peer in [left, right] + peers1 + peers2:
        pl.semaphore_signal(barrier, inc=1, device_id=(peer,), device_id_type=MESH)
    pl.semaphore_wait(barrier, 2 + 15 + groups - 1)

    def remote(src, dst, send, recv, peer):
        copy = pltpu.make_async_remote_copy(
            src_ref=src, dst_ref=dst, send_sem=send, recv_sem=recv, device_id=(peer,), device_id_type=MESH
        )
        copy.start()
        return copy

    mine = pltpu.make_async_copy(region, table.at[pl.ds(me, 1)], own.at[0])
    mine.start()
    first = [
        remote(region, table.at[pl.ds(me, 1)], g1_s.at[k], g1_r.at[k], peer) for k, peer in enumerate(peers1)
    ]
    halo = [
        remote(packed.at[:, pl.ds(0, 128)], hc.at[0], cf_s.at[0], cf_r.at[0], right),
        remote(packed.at[:, pl.ds(0, 128)], hc.at[1], cf_s.at[1], cf_r.at[1], left),
        remote(xm.at[3], hx.at[0], px_s.at[0], px_r.at[0], right),
        remote(xm.at[0], hx.at[1], px_s.at[1], px_r.at[1], left),
    ]
    mine.wait()
    for copy in first:
        copy.wait()
    block = table.at[pl.ds(group * 16, 16)]
    second = [remote(block, block, g2_s.at[k], g2_r.at[k], peer) for k, peer in enumerate(peers2)]
    for copy in second:
        copy.wait()
    for copy in halo:
        copy.wait()


def top_blocks(me, offset_t, top_c):
    bases = (0, 256, 384, 448)
    lane = iota((8, 480), 1)
    offsets = offset_t[...].astype(F32)
    picks = []
    for h in range(4):
        chosen = jnp.sum(jnp.where(lane == bases[h] + (me >> h), offsets, 0.0), 1, keepdims=True)
        picks.append((iota((8, 160), 1).astype(F32) == chosen).astype(F32))
    pick = jnp.concatenate(picks, 0).astype(BF16)
    hi, lo = split(top_c[...].reshape(1024, 160))
    return dot(hi, pick, NT) + dot(lo, pick, NT)


def top_expand(me, table, partner_t, count, blocks, paths, path_ref):
    both, two, three, _ = paths
    bases = (0, 256, 384, 448)
    lane = iota((8, 480), 1)
    slot = iota((8, 256), 0)
    partners = partner_t[...].astype(F32)
    node = iota((8, 256), 1).astype(F32)
    picks = []
    for h in range(4):
        row = bases[h] + (me >> h)
        chosen = jnp.sum(jnp.where(lane == row, partners, 0.0), 1, keepdims=True) - bases[h]
        live = slot < count[row]
        for t in range(2**h):
            picks.append(jnp.where(live & (node == chosen * 2**h + t), 1.0, 0.0))
    pick = jnp.concatenate(picks, 0).astype(BF16)
    hi, lo = split(table)
    picked = dot(pick, hi) + dot(pick, lo)
    stacks = (None, both, two, three)
    first = 0
    nodes = [[], []]
    for h in range(4):
        merged = []
        for rhs in range(2):
            merged.append(
                jnp.concatenate(
                    [
                        picked[first + 8 * t : first + 8 * t + 8, rhs * 32 : rhs * 32 + 32]
                        for t in range(2**h)
                    ],
                    1,
                )
            )
        merged = jnp.concatenate(merged, 0)
        if h > 0:
            merged = dot3(merged, stacks[h])
        nodes[0].append(merged[0:8])
        nodes[1].append(merged[8:16])
        first += 8 * 2**h
    local = []
    for rhs in range(2):
        across = jnp.concatenate(nodes[rhs], 0).T
        total = jnp.zeros((32, 32), F32)
        for a in range(32):
            total = total + blocks[32 * a : 32 * a + 32] * across[a : a + 1]
        total = total.T
        local.append([jnp.sum(total[8 * h : 8 * h + 8], 0, keepdims=True) for h in range(4)])
    path_ref[0:64, 0:32] = both
    path_ref[64:192, 0:32] = two
    path_ref[192:448, 0:32] = three
    expansion = jnp.concatenate([local[0][0], local[1][0]] * 4, 0)
    starts = (0, 0, 64, 192)
    for h in range(1, 4):
        here = jnp.concatenate([local[0][h], local[1][h]] * 4, 0)
        begin = pl.multiple_of(starts[h] + (me & (2**h - 1)) * 32, 32)
        path = path_ref[pl.ds(begin, 32), :][:, 0:32]
        expansion = expansion + dot3(here, path, NT)
    return expansion[0:2]


def descend(expansion, v_ref, w_ref, paths):
    _, _, three, four = paths
    wide = dot3(jnp.concatenate([expansion] * 4, 0), four, NT)[0:2]
    for a in range(16):
        w_ref[pl.ds(a, 2, stride=16), 0:32] = wide[:, 32 * a : 32 * a + 32]
    wide = dot3(w_ref[:, 0:32], four, NT)
    for rhs in range(2):
        for b in range(16):
            v_ref[pl.ds(2 * b + rhs, 16, stride=32), 0:32] = wide[
                16 * rhs : 16 * rhs + 16, 32 * b : 32 * b + 32
            ]
    merge = jnp.concatenate(
        [
            three[(c * 4 + i) * 32 : (c * 4 + i) * 32 + 32]
            for i in (3, 2, 1, 0)
            for c in (1, 0)
        ],
        0,
    )
    return dot3(v_ref[:, 0:32], merge, NT)


def offset_number(a, b):
    if max(abs(a), abs(b)) < 2 or max(abs(a), abs(b)) > 3:
        return None
    number = 0
    for x in range(-3, 4):
        for y in range(-3, 4):
            if (x, y) == (a, b):
                return number
            if max(abs(x), abs(y)) >= 2:
                number += 1


BETAS = (-2, -1, 0, 1, 2, 3, 4, -3)
ROW_GROUPS = ((1, 2, 0, 3), (-3, -2, 5, 6, -1, 4))


def far_weights(coupling, window, w_hi, w_lo):
    window[...] = jnp.zeros_like(window)
    for at, beta in enumerate(BETAS):
        for a in range(-3, 4):
            for side in range(2):
                number = offset_number(a, beta - 1 + side)
                if number is not None:
                    block = coupling[number]
                    start = (a + 6) * 64 + side * 32
                    window[0, at, :, start : start + 32] = block
                    window[1, at, :, start + 64 : start + 96] = block
    row = 0
    for shift in range(4):
        for i in ROW_GROUPS[0] + ROW_GROUPS[1]:
            for c in range(2):
                start = (i + 3) * 64
                odd = (start // 64) % 2
                part = window[odd, 2 * shift + c, :, start + 64 * odd : start + 64 * odd + 256]
                hi, lo = split(part)
                w_hi[row : row + 32] = hi
                w_lo[row : row + 32] = lo
                row += 32


def far_field(coef, w_hi, w_lo, far):
    chunk = 128
    lane = iota((chunk, 640), 1)
    even = (lane & 32) == 0
    for m in range(512 // chunk):
        at = 8 + m * chunk
        views = [coef[pl.ds(at + 2 * d, chunk)] for d in (-1, 0, 1)]
        views.append(jnp.where(even, coef[pl.ds(at + 4, chunk)], coef[pl.ds(at - 4, chunk)]))
        parts = [split(view) for view in views]
        hi = jnp.concatenate([part[0] for part in parts], 1)
        lo = jnp.concatenate([part[1] for part in parts], 1)
        far[pl.ds(m * chunk, chunk)] = dot(hi, w_hi[...]) + dot(lo, w_hi[...]) + dot(hi, w_lo[...])


def kernel_down(
    n, xm, hx, packed, hc, table, mcol, bt, near, transfer, coupling, top_c, partner_t, offset_t, count, out,
    taps, coef, window, w_hi, w_lo, far, v_ref, w_ref, path_ref, weight, os, sem
):
    me = lax.axis_index("region")
    is_first = jnp.where(me > 0, 1.0, 0.0)
    is_last = jnp.where(me < n - 1, 1.0, 0.0)
    paths = tree_paths(transfer)
    blocks = top_blocks(me, offset_t, top_c)
    expansion = top_expand(me, table.reshape(256, 128)[...], partner_t, count, blocks, paths, path_ref)
    leaf = descend(expansion, v_ref, w_ref, paths)
    far_weights(coupling, window, w_hi, w_lo)
    hx0 = [hx[0, c] * is_first.astype(BF16) for c in range(2)]
    hx1 = [hx[1, c] * is_last.astype(BF16) for c in range(2)]
    zero8 = jnp.zeros((8, 640), F32)
    coef[0:8] = zero8
    coef[520:528] = zero8
    coef[8:520, 0:256] = packed[...]
    coef[8:520, 256:384] = hc[0] * is_first
    coef[8:520, 384:512] = hc[1] * is_last
    basis = bt[...]
    for k, rows in enumerate((hx0, hx1)):
        for c in range(2):
            start = 512 + 64 * k + 32 * c
            coef[8:520, start : start + 32] = dot(rows[c], basis, NT)
    far_field(coef, w_hi, w_lo, far)
    leaf = leaf + far[...]
    hi, lo = split(leaf)
    for r in range(6):
        rows = hx0 if r == 0 else hx1 if r == 5 else [xm[r - 1, 0], xm[r - 1, 1]]
        taps[r, 0, 16:528] = rows[0]
        taps[r, 1, 16:528] = rows[1]
        taps[r, 0, 528:544] = jnp.zeros((16, 256), BF16)
        taps[r, 1, 0:16] = jnp.zeros((16, 256), BF16)
        taps[r, 2, 16:528] = taps[r, 0, 18:530]
        taps[r, 3, 16:528] = taps[r, 1, 14:526]
    order = ((3, 0, 1), (0, 1, 2))
    weight[...] = jnp.zeros_like(weight)
    for i2 in range(2):
        for c in range(2):
            start = (1 - i2) * 64 + (1 - c) * 32
            weight[i2, c, pl.ds(start, 32)] = basis
            weight[i2, c, pl.ds(128 + start, 32)] = basis
    copies = []
    chunk = 256
    for i in range(4):
        for c in range(2):
            half = 0 if i >= 2 else 128
            for m in range(512 // chunk):
                rows = pl.ds(16 + m * chunk, chunk)
                parts = [taps[i + a, order[c][b], rows] for a in range(3) for b in range(3)]
                acc = dot(jnp.concatenate(parts, 1), near[...])
                tail = slice(m * chunk, (m + 1) * chunk)
                exps = jnp.concatenate([hi[tail, half : half + 128], lo[tail, half : half + 128]], 1)
                acc = acc + dot(exps, weight[i % 2, c])
                col = mcol[i, c, pl.ds(m * chunk, chunk)].astype(F32)
                for lt in range(2):
                    os.at[i, c, lt].reshape(512, 128)[pl.ds(m * chunk, chunk)] = (
                        acc[:, lt * 128 : lt * 128 + 128] * col
                    )
            for lt in range(2):
                copy = pltpu.make_async_copy(
                    os.at[i, c, lt], out.at[i, :, c, :, pl.ds(lt * 128, 128)], sem.at[i, c, lt]
                )
                copy.start()
                copies.append(copy)
    for copy in copies:
        copy.wait()


def body(n, pixels, valid, basis, near, transfer, coupling, top_c, partner, offset, count):
    x = pixels.reshape(4, 256, 2, 2, 256)
    bt = basis.T
    vmem = pl.BlockSpec(memory_space=pltpu.VMEM)
    anywhere = pl.BlockSpec(memory_space=pl.ANY)
    sds = jax.ShapeDtypeStruct
    dma = pltpu.SemaphoreType.DMA
    xm, mcol, packed, region = pl.pallas_call(
        kernel_up,
        out_shape=(sds((4, 2, 512, 256), BF16), sds((4, 2, 512, 128), BF16), sds((512, 256), F32), sds((1, 1, 128), F32)),
        in_specs=[anywhere, vmem, vmem, vmem],
        out_specs=(vmem, vmem, vmem, vmem),
        scratch_shapes=[
            pltpu.VMEM((4, 2, 2, 256, 2, 128), BF16),
            pltpu.VMEM((256, 2048), BF16),
            pltpu.VMEM((512, 128), F32),
            pltpu.VMEM((32, 128), F32),
            dma((4, 2, 2)),
        ],
        compiler_params=pltpu.CompilerParams(vmem_limit_bytes=VMEM_LIMIT),
    )(x, valid, bt, transfer)
    hx, hc, table = pl.pallas_call(
        functools.partial(kernel_move, n),
        out_shape=(sds((2, 2, 512, 256), BF16), sds((2, 512, 128), F32), sds((n, 1, 128), F32)),
        in_specs=[anywhere] * 3,
        out_specs=(anywhere,) * 3,
        scratch_shapes=[dma((2,)), dma((2,)), dma((2,)), dma((2,)), dma((15,)), dma((15,)), dma((n // 16 - 1,)), dma((n // 16 - 1,)), dma((1,))],
        compiler_params=pltpu.CompilerParams(collective_id=0, has_side_effects=True),
    )(xm, packed, region)
    out = pl.pallas_call(
        functools.partial(kernel_down, n),
        out_shape=sds((4, 256, 2, 2, 256), F32),
        in_specs=[vmem] * 13 + [pl.BlockSpec(memory_space=pltpu.SMEM)],
        out_specs=anywhere,
        scratch_shapes=[
            pltpu.VMEM((6, 4, 544, 256), BF16),
            pltpu.VMEM((528, 640), F32),
            pltpu.VMEM((2, 8, 32, 1024), F32),
            pltpu.VMEM((2560, 256), BF16),
            pltpu.VMEM((2560, 256), BF16),
            pltpu.VMEM((512, 256), F32),
            pltpu.VMEM((512, 128), F32),
            pltpu.VMEM((32, 128), F32),
            pltpu.VMEM((448, 128), F32),
            pltpu.VMEM((2, 2, 256, 256), BF16),
            pltpu.VMEM((4, 2, 2, 256, 2, 128), F32),
            dma((4, 2, 2)),
        ],
        compiler_params=pltpu.CompilerParams(vmem_limit_bytes=VMEM_LIMIT),
    )(
        xm, hx, packed, hc, table, mcol, bt, near.reshape(2304, 256), transfer, coupling,
        jnp.transpose(top_c, (1, 2, 0)), partner.T, offset.T, count,
    )
    return out.reshape(4, 512, 2, 256)


def solution(mesh):
    n = mesh.shape["region"]
    in_specs = (P("region", None, None, None), P("region", None)) + (P(),) * 8
    out_specs = P("region", None, None, None)
    return jax.shard_map(functools.partial(body, n), mesh=mesh, in_specs=in_specs, out_specs=out_specs, check_vma=False)
```

profile of v0, /device:TPU:1, one launch (start us, length us, event | category | flops | bytes accessed | tf_op | source)
XLA Modules:
  0.0 54.0 jit_solution(3853721213694810147)
XLA Ops:
  0.0 2.4 %copy.11.coupling = f32[40,32,32]{2,1,0:T(8,128)} copy(f32[40,32,32]{0,2,1:T(8,128)} %param.15) | data formatting | bytes 327680 | tf_op args[5]
  2.4 7.1 %shard_map.100 = (bf16[4,2,512,256]{3,2,1,0:T(8,128)(2,1)}, bf16[4,2,512,128]{3,2,1,0:T(8,128)(2,1)}, f32[512,256]{1,0:T(8,128)}, f32[1,1,128]{2,1,0:T(1,128)}) custom-call(bf16[4,256,2,2,256]{4,3,2,1,0:T(2,128)(2,1)} %bitcast.7, s32[4,512]{1,0:T(4,128)} %valid.1, bf16[32,256]{1,0:T(8,128)(2,1)} %bitcast.10, f32[2,32,32]{2,1,0:T(8,128)} %transfer.3), custom_call_target="tpu_custom_call" | custom-call | tf_op jit(solution)/shard_map/pallas_call | solution.py:382
  9.5 26.0 %shard_map.101 = (bf16[2,2,512,256]{3,2,1,0:T(8,128)(2,1)}, f32[2,512,128]{2,1,0:T(8,128)}, f32[256,1,128]{2,1,0:T(1,128)}) custom-call(bf16[4,2,512,256]{3,2,1,0:T(8,128)(2,1)} %get-tuple-element.12.xm, f32[512,256]{1,0:T(8,128)} %get-tuple-element.13.packed, f32[1,1,128]{2,1,0:T(1,128)} %get-tuple-element.14.region), custom_call_target="tpu_custom_call" | custom-call | tf_op jit(solution)/shard_map/pallas_call | solution.py:396
  35.5 18.3 %shard_map.102 = f32[4,256,2,2,256]{4,3,2,1,0:T(2,128)} custom-call(bf16[4,2,512,256]{3,2,1,0:T(8,128)(2,1)} %get-tuple-element.12.xm, bf16[2,2,512,256]{3,2,1,0:T(8,128)(2,1)} %get-tuple-element.15.hx, f32[512,256]{1,0:T(8,128)} %get-tuple-element.13.packed, f32[2,512,128]{2,1,0:T(8,128)} %get-tuple-element.16.hc, f32[256,1,128]{2,1,0:T(1,128)} %get-tuple-element.17.table, ...), custom_call_target="tpu_custom_call" | custom-call | tf_op jit(solution)/shard_map/pallas_call | solution.py:404
where the time goes:
time: 54.2 us; the launch traced here: 54 us
  Pallas kernels  51.4 us (95%)
  local copies, waits for them, and re-layouts  2.41 us (4%)
    pallas_call x1, Pallas kernels, body(): pl.pallas_call(functools.partial(kernel_move, n), out_shape=(sds((2, 2, 5...  26 us
    pallas_call x1, Pallas kernels, body(): pl.pallas_call(functools.partial(kernel_down, n), out_shape=sds((4, 256,...  18.3 us
    pallas_call x1, Pallas kernels, body(): pl.pallas_call(kernel_up, out_shape=(sds((4, 2, 512, 256), BF16), sds((4,...  7.1 us
    unnamed x1, local copies, waits for them, and re-layouts  2.41 us

commit v1 on v0

v1 whole, which is shorter than its diff:
```python
import functools

import jax
import jax.numpy as jnp
from jax import lax
from jax.experimental import pallas as pl
from jax.experimental.pallas import tpu as pltpu
from jax.sharding import PartitionSpec as P

MESH = pl.DeviceIdType.MESH
F32 = jnp.float32
BF16 = jnp.bfloat16
NN = (((1,), (0,)), ((), ()))
NT = (((1,), (1,)), ((), ()))
IN_ORDER = (1, 2, 0, 3)
VMEM_LIMIT = 56 << 20


def dot(a, b, dims=NN):
    return lax.dot_general(a, b, dims, preferred_element_type=F32)


def split(x):
    hi = x.astype(BF16)
    return hi, (x - hi.astype(F32)).astype(BF16)


def dot3(a, b, dims=NN):
    a_hi, a_lo = split(a)
    b_hi, b_lo = split(b)
    return dot(a_hi, b_hi, dims) + (dot(a_lo, b_hi, dims) + dot(a_hi, b_lo, dims))


def iota(shape, axis):
    return lax.broadcasted_iota(jnp.int32, shape, axis)


def local(src, dst, sem):
    copy = pltpu.make_async_copy(src, dst, sem)
    copy.start()
    return copy


def await_bytes(ref, sem):
    pltpu.make_async_copy(ref, ref, sem).wait()


def tree_paths(transfer):
    side0, side1 = transfer[0], transfer[1]
    both = jnp.concatenate([side0, side1], 0)
    lanes = jnp.concatenate([side0, side1], 1)
    pairs = dot3(both, lanes)
    two = jnp.concatenate([pairs[:, :32], pairs[:, 32:]], 0)
    three = dot3(two, lanes)
    three = jnp.concatenate([three[:, :32], three[:, 32:]], 0)
    two_lanes = jnp.concatenate([two[32 * s : 32 * s + 32] for s in range(4)], 1)
    four = dot3(two, two_lanes)
    four = jnp.concatenate([four[:, 32 * s : 32 * s + 32] for s in range(4)], 0)
    return both, two, three, four


def mask_rows(valid):
    values = valid.astype(F32).astype(BF16)
    values = jnp.concatenate([values, values], 0)
    lane = iota((512, 1024), 1)
    leaf = (lane & 510) + (lane >> 9)
    pick = (iota((512, 1024), 0) == leaf).astype(F32).astype(BF16)
    return dot(values, pick)


def column(row):
    return jnp.concatenate(
        [jnp.broadcast_to(row[:, 128 * b : 128 * b + 128], (128, 128)).T for b in range(4)], 0
    )


def climb(packed, v_ref, w_ref, paths):
    _, _, three, four = paths
    merge = jnp.concatenate(
        [three[(c * 4 + i) * 32 : (c * 4 + i) * 32 + 32] for i in IN_ORDER for c in range(2)], 0
    )
    v_ref[:, 0:32] = dot3(packed, merge)
    rows = []
    for rhs in range(2):
        rows.append(
            jnp.concatenate(
                [v_ref[pl.ds(2 * b + rhs, 16, stride=32), :][:, 0:32] for b in range(16)], 1
            )
        )
    w_ref[:, 0:32] = dot3(jnp.concatenate(rows, 0), four)
    last = jnp.concatenate([w_ref[pl.ds(a, 2, stride=16), :][:, 0:32] for a in range(16)], 1)
    return dot3(jnp.concatenate([last, last, last, last], 0), four)[0:2]


def top_blocks(me, offset_t, top_c):
    bases = (0, 256, 384, 448)
    lane = iota((8, 480), 1)
    offsets = offset_t[...].astype(F32)
    picks = []
    for h in range(4):
        chosen = jnp.sum(jnp.where(lane == bases[h] + (me >> h), offsets, 0.0), 1, keepdims=True)
        picks.append((iota((8, 160), 1).astype(F32) == chosen).astype(F32))
    pick = jnp.concatenate(picks, 0).astype(BF16)
    hi, lo = split(top_c[...].reshape(1024, 160))
    return dot(hi, pick, NT) + dot(lo, pick, NT)


def top_expand(me, table, partner_t, count, blocks, paths, path_ref):
    both, two, three, _ = paths
    bases = (0, 256, 384, 448)
    lane = iota((8, 480), 1)
    slot = iota((8, 256), 0)
    partners = partner_t[...].astype(F32)
    node = iota((8, 256), 1).astype(F32)
    picks = []
    for h in range(4):
        row = bases[h] + (me >> h)
        chosen = jnp.sum(jnp.where(lane == row, partners, 0.0), 1, keepdims=True) - bases[h]
        live = slot < count[row]
        for t in range(2**h):
            picks.append(jnp.where(live & (node == chosen * 2**h + t), 1.0, 0.0))
    pick = jnp.concatenate(picks, 0).astype(BF16)
    hi, lo = split(table)
    picked = dot(pick, hi) + dot(pick, lo)
    stacks = (None, both, two, three)
    first = 0
    nodes = [[], []]
    for h in range(4):
        merged = []
        for rhs in range(2):
            merged.append(
                jnp.concatenate(
                    [
                        picked[first + 8 * t : first + 8 * t + 8, rhs * 32 : rhs * 32 + 32]
                        for t in range(2**h)
                    ],
                    1,
                )
            )
        merged = jnp.concatenate(merged, 0)
        if h > 0:
            merged = dot3(merged, stacks[h])
        nodes[0].append(merged[0:8])
        nodes[1].append(merged[8:16])
        first += 8 * 2**h
    local = []
    for rhs in range(2):
        across = jnp.concatenate(nodes[rhs], 0).T
        total = jnp.zeros((32, 32), F32)
        for a in range(32):
            total = total + blocks[32 * a : 32 * a + 32] * across[a : a + 1]
        total = total.T
        local.append([jnp.sum(total[8 * h : 8 * h + 8], 0, keepdims=True) for h in range(4)])
    path_ref[0:64, 0:32] = both
    path_ref[64:192, 0:32] = two
    path_ref[192:448, 0:32] = three
    expansion = jnp.concatenate([local[0][0], local[1][0]] * 4, 0)
    starts = (0, 0, 64, 192)
    for h in range(1, 4):
        here = jnp.concatenate([local[0][h], local[1][h]] * 4, 0)
        begin = pl.multiple_of(starts[h] + (me & (2**h - 1)) * 32, 32)
        path = path_ref[pl.ds(begin, 32), :][:, 0:32]
        expansion = expansion + dot3(here, path, NT)
    return expansion[0:2]


def descend(expansion, v_ref, w_ref, paths):
    _, _, three, four = paths
    wide = dot3(jnp.concatenate([expansion] * 4, 0), four, NT)[0:2]
    for a in range(16):
        w_ref[pl.ds(a, 2, stride=16), 0:32] = wide[:, 32 * a : 32 * a + 32]
    wide = dot3(w_ref[:, 0:32], four, NT)
    for rhs in range(2):
        for b in range(16):
            v_ref[pl.ds(2 * b + rhs, 16, stride=32), 0:32] = wide[
                16 * rhs : 16 * rhs + 16, 32 * b : 32 * b + 32
            ]
    merge = jnp.concatenate(
        [
            three[(c * 4 + i) * 32 : (c * 4 + i) * 32 + 32]
            for i in (3, 2, 1, 0)
            for c in (1, 0)
        ],
        0,
    )
    return dot3(v_ref[:, 0:32], merge, NT)


OFFSETS = [(a, b) for a in range(-3, 4) for b in range(-3, 4) if max(abs(a), abs(b)) >= 2]
BETAS = (-2, -1, 0, 1, 2, 3, 4, -3)
ROW_GROUPS = ((1, 2, 0, 3), (-3, -2, 5, 6, -1, 4))


def far_weights(coupling, blocks, window, w_hi, w_lo):
    for k in range(32):
        blocks[pl.ds(40 * k, 40), 0:32] = coupling[k].T
    window[...] = jnp.zeros_like(window)
    for number, (a, b) in enumerate(OFFSETS):
        block = blocks[pl.ds(number, 32, stride=40), :][:, 0:32]
        for at, beta in enumerate(BETAS):
            for side in range(2):
                if beta - 1 + side == b:
                    start = (a + 6) * 64 + side * 32
                    window[0, at, :, start : start + 32] = block
                    window[1, at, :, start + 64 : start + 96] = block
    row = 0
    for group in ROW_GROUPS:
        for shift in range(4):
            for i in group:
                for c in range(2):
                    start = (i + 3) * 64
                    odd = (start // 64) % 2
                    part = window[odd, 2 * shift + c, :, start + 64 * odd : start + 64 * odd + 256]
                    hi, lo = split(part)
                    w_hi[row : row + 32] = hi
                    w_lo[row : row + 32] = lo
                    row += 32


def far_field(coef, first, w_hi, w_lo, far):
    chunk = 128
    lanes = coef.shape[1]
    even = (iota((chunk, lanes), 1) & 32) == 0
    weights = pl.ds(first, 4 * lanes)
    for m in range(512 // chunk):
        at = 8 + m * chunk
        views = [coef[pl.ds(at + 2 * d, chunk)] for d in (-1, 0, 1)]
        views.append(jnp.where(even, coef[pl.ds(at + 4, chunk)], coef[pl.ds(at - 4, chunk)]))
        parts = [split(view) for view in views]
        hi = jnp.concatenate([part[0] for part in parts], 1)
        lo = jnp.concatenate([part[1] for part in parts], 1)
        total = dot(hi, w_hi[weights]) + dot(lo, w_hi[weights]) + dot(hi, w_lo[weights])
        rows = pl.ds(m * chunk, chunk)
        far[rows] = total if first == 0 else far[rows] + total


ORDER = ((3, 0, 1), (0, 1, 2))
CHUNK = 256


def shifted(taps, r):
    taps[r, 0, 528:544] = jnp.zeros((16, 256), BF16)
    taps[r, 1, 0:16] = jnp.zeros((16, 256), BF16)
    taps[r, 2, 16:528] = taps[r, 0, 18:530]
    taps[r, 3, 16:528] = taps[r, 1, 14:526]


def near_rows(taps, near, acc, i, rows, add):
    first, count = rows[0], len(rows)
    for c in range(2):
        for m in range(512 // CHUNK):
            span = pl.ds(16 + m * CHUNK, CHUNK)
            parts = [taps[i + a, ORDER[c][b], span] for a in rows for b in range(3)]
            total = dot(jnp.concatenate(parts, 1), near[pl.ds(768 * first, 768 * count)])
            out = pl.ds(m * CHUNK, CHUNK)
            acc[i, c, out] = acc[i, c, out] + total if add else total


def kernel_main(
    n, x, near_any, coupling_any, top_any, valid, bt, transfer, partner_t, offset_t, count, acc_out, exp_out, mcol_out,
    xs, near, coupling, top_c, mcol, taps, basis, packed, coef, coef_halo, hc, table, blocks, window, w_hi, w_lo, far,
    acc, exps, v_ref, w_ref, path_ref, x_sem, w_sem, px_s, px_r, cf_s, cf_r, g_s, g_r, o_sem
):
    me = lax.axis_index("region")
    right, left = lax.rem(me + 1, n), lax.rem(me + n - 1, n)
    group = me // 16
    spot = lax.rem(me, 16)
    groups = n // 16
    barrier = pltpu.get_barrier_semaphore()
    peers1 = [group * 16 + lax.rem(spot + k, 16) for k in range(1, 16)]
    peers2 = [lax.rem(group + k, groups) * 16 + spot for k in range(1, groups)]

    def remote(src, dst, send, recv, peer):
        copy = pltpu.make_async_remote_copy(
            src_ref=src, dst_ref=dst, send_sem=send, recv_sem=recv, device_id=(peer,), device_id_type=MESH
        )
        copy.start()
        return copy

    for peer in [left, right] + peers1 + peers2:
        pl.semaphore_signal(barrier, inc=1, device_id=(peer,), device_id_type=MESH)
    for i in (0, 3, 1, 2):
        for c in range(2):
            for lt in range(2):
                local(x.at[i, :, c, :, pl.ds(lt * 128, 128)], xs.at[i, c, lt], x_sem.at[i])
    near_load = local(near_any, near, w_sem.at[0])
    coupling_load = local(coupling_any, coupling, w_sem.at[1])
    top_load = local(top_any, top_c, w_sem.at[2])

    basis[...] = jnp.zeros_like(basis)
    for at, i in enumerate(IN_ORDER):
        for c in range(2):
            basis[pl.ds(at * 64 + c * 32, 32), pl.ds((i * 2 + c) * 256, 256)] = bt[...]
    paths = tree_paths(transfer)
    rows = mask_rows(valid[...])
    for i in (0, 3, 1, 2):
        await_bytes(xs.at[i], x_sem.at[i])
        for c in range(2):
            col = column(rows[i : i + 1, c * 512 : c * 512 + 512]).astype(BF16)
            mcol[i, c] = col
            for lt in range(2):
                part = xs.at[i, c, lt].reshape(512, 128)[...]
                taps[i + 1, c, 16:528, lt * 128 : lt * 128 + 128] = part * col
    mcol_copy = local(mcol, mcol_out, o_sem.at[0])
    pixels = jnp.concatenate([taps[i + 1, c, 16:528] for i in range(4) for c in range(2)], 1)
    packed[...] = dot(pixels, basis[...], NT)
    top = climb(packed[...], v_ref, w_ref, paths)
    table[pl.ds(me, 1)] = jnp.concatenate([top[0:1], top[1:2], jnp.zeros((1, 64), F32)], 1).reshape(1, 1, 128)

    pl.semaphore_wait(barrier, 2 + 15 + groups - 1)
    mine = table.at[pl.ds(me, 1)]
    for peer in peers1:
        remote(mine, mine, g_s.at[0], g_r.at[0], peer)
    sent = packed.at[:, pl.ds(0, 128)]
    coef_copies = [
        remote(sent, hc.at[0], cf_s.at[0], cf_r.at[0], right),
        remote(sent, hc.at[1], cf_s.at[1], cf_r.at[1], left),
    ]
    inside = pl.ds(16, 512)
    pixel_copies = [
        remote(taps.at[4, pl.ds(0, 2), inside], taps.at[0, pl.ds(0, 2), inside], px_s.at[0], px_r.at[0], right),
        remote(taps.at[1, pl.ds(0, 2), inside], taps.at[5, pl.ds(0, 2), inside], px_s.at[1], px_r.at[1], left),
    ]

    for r in range(1, 5):
        shifted(taps, r)
    near_load.wait()
    near_rows(taps, near, acc, 1, (0, 1, 2), False)
    near_rows(taps, near, acc, 2, (0, 1, 2), False)

    await_bytes(table.at[pl.ds(0, 15)], g_s.at[0])
    await_bytes(table.at[pl.ds(0, 15)], g_r.at[0])
    block = table.at[pl.ds(group * 16, 16)]
    for peer in peers2:
        remote(block, block, g_s.at[1], g_r.at[1], peer)

    inner_copy = local(acc.at[pl.ds(1, 2)], acc_out.at[pl.ds(1, 2)], o_sem.at[1])
    coupling_load.wait()
    far_weights(coupling, blocks, window, w_hi, w_lo)
    top_load.wait()
    slots = top_blocks(me, offset_t, top_c)
    coef[0:8] = jnp.zeros((8, 256), F32)
    coef[520:528] = jnp.zeros((8, 256), F32)
    coef[8:520] = packed[...]
    far_field(coef, 0, w_hi, w_lo, far)
    near_rows(taps, near, acc, 0, (1, 2), False)
    near_rows(taps, near, acc, 3, (0, 1), False)

    for copy in pixel_copies:
        copy.wait()

    @pl.when(me == 0)
    def _():
        taps[0, 0:2, 16:528] = jnp.zeros((2, 512, 256), BF16)

    @pl.when(me == n - 1)
    def _():
        taps[5, 0:2, 16:528] = jnp.zeros((2, 512, 256), BF16)

    shifted(taps, 0)
    shifted(taps, 5)
    near_rows(taps, near, acc, 0, (0,), True)
    near_rows(taps, near, acc, 3, (2,), True)
    outer_copies = [local(acc.at[i], acc_out.at[i], o_sem.at[k]) for k, i in ((2, 0), (3, 3))]

    for copy in coef_copies:
        copy.wait()
    coef_halo[0:8] = jnp.zeros((8, 384), F32)
    coef_halo[520:528] = jnp.zeros((8, 384), F32)
    coef_halo[8:520, 0:128] = hc[0] * jnp.where(me > 0, 1.0, 0.0)
    coef_halo[8:520, 128:256] = hc[1] * jnp.where(me < n - 1, 1.0, 0.0)
    for k, r in enumerate((0, 5)):
        for c in range(2):
            start = 256 + 64 * k + 32 * c
            coef_halo[8:520, start : start + 32] = dot(taps[r, c, 16:528], bt[...], NT)
    far_field(coef_halo, 1024, w_hi, w_lo, far)

    await_bytes(table.at[pl.ds(0, n - 16)], g_s.at[1])
    await_bytes(table.at[pl.ds(0, n - 16)], g_r.at[1])
    expansion = top_expand(me, table.reshape(n, 128)[...], partner_t, count, slots, paths, path_ref)
    leaf = descend(expansion, v_ref, w_ref, paths) + far[...]
    hi, lo = split(leaf)
    for half in range(2):
        exps[half, :, 0:128] = hi[:, half * 128 : half * 128 + 128]
        exps[half, :, 128:256] = lo[:, half * 128 : half * 128 + 128]
    exp_copy = local(exps, exp_out, o_sem.at[4])
    for copy in [mcol_copy, inner_copy] + outer_copies + [exp_copy]:
        copy.wait()


def kernel_out(acc_any, exps, mcol_any, bt, out, acc, mcol, weight, os, in_sem, out_sem):
    loads = [
        (local(acc_any.at[i, c], acc.at[i, c], in_sem.at[i, c]), local(mcol_any.at[i, c], mcol.at[i, c], in_sem.at[4 + i, c]))
        for i in range(4)
        for c in range(2)
    ]
    weight[...] = jnp.zeros_like(weight)
    for i2 in range(2):
        for c in range(2):
            start = (1 - i2) * 64 + (1 - c) * 32
            weight[i2, c, pl.ds(start, 32)] = bt[...]
            weight[i2, c, pl.ds(128 + start, 32)] = bt[...]
    for i in range(4):
        for c in range(2):
            for copy in loads[i * 2 + c]:
                copy.wait()
            total = acc[i, c] + dot(exps[1 - i // 2], weight[i % 2, c])
            col = mcol[i, c].astype(F32)
            for lt in range(2):
                os.at[i, c, lt].reshape(512, 128)[...] = total[:, lt * 128 : lt * 128 + 128] * col
                local(os.at[i, c, lt], out.at[i, :, c, :, pl.ds(lt * 128, 128)], out_sem.at[0])
    await_bytes(os, out_sem.at[0])


def body(n, pixels, valid, basis, near, transfer, coupling, top_c, partner, offset, count):
    x = pixels.reshape(4, 256, 2, 2, 256)
    bt = basis.T
    vmem = pl.BlockSpec(memory_space=pltpu.VMEM)
    anywhere = pl.BlockSpec(memory_space=pl.ANY)
    sds = jax.ShapeDtypeStruct
    dma = pltpu.SemaphoreType.DMA
    acc, exps, mcol = pl.pallas_call(
        functools.partial(kernel_main, n),
        out_shape=(sds((4, 2, 512, 256), F32), sds((2, 512, 256), BF16), sds((4, 2, 512, 128), BF16)),
        in_specs=[anywhere] * 4 + [vmem] * 5 + [pl.BlockSpec(memory_space=pltpu.SMEM)],
        out_specs=(anywhere,) * 3,
        scratch_shapes=[
            pltpu.VMEM((4, 2, 2, 256, 2, 128), BF16),
            pltpu.VMEM((2304, 256), BF16),
            pltpu.VMEM((32, 32, 40), F32),
            pltpu.VMEM((32, 32, 160), F32),
            pltpu.VMEM((4, 2, 512, 128), BF16),
            pltpu.VMEM((6, 4, 544, 256), BF16),
            pltpu.VMEM((256, 2048), BF16),
            pltpu.VMEM((512, 256), F32),
            pltpu.VMEM((528, 256), F32),
            pltpu.VMEM((528, 384), F32),
            pltpu.VMEM((2, 512, 128), F32),
            pltpu.VMEM((n, 1, 128), F32),
            pltpu.VMEM((1280, 128), F32),
            pltpu.VMEM((2, 8, 32, 1024), F32),
            pltpu.VMEM((2560, 256), BF16),
            pltpu.VMEM((2560, 256), BF16),
            pltpu.VMEM((512, 256), F32),
            pltpu.VMEM((4, 2, 512, 256), F32),
            pltpu.VMEM((2, 512, 256), BF16),
            pltpu.VMEM((512, 128), F32),
            pltpu.VMEM((32, 128), F32),
            pltpu.VMEM((448, 128), F32),
            dma((4,)),
            dma((3,)),
            dma((2,)),
            dma((2,)),
            dma((2,)),
            dma((2,)),
            dma((2,)),
            dma((2,)),
            dma((5,)),
        ],
        compiler_params=pltpu.CompilerParams(collective_id=0, has_side_effects=True, vmem_limit_bytes=VMEM_LIMIT),
    )(
        x, near.reshape(2304, 256), jnp.transpose(coupling, (1, 2, 0)), jnp.transpose(top_c, (1, 2, 0)),
        valid, bt, transfer, partner.T, offset.T, count,
    )
    out = pl.pallas_call(
        kernel_out,
        out_shape=sds((4, 256, 2, 2, 256), F32),
        in_specs=[anywhere, vmem, anywhere, vmem],
        out_specs=anywhere,
        scratch_shapes=[
            pltpu.VMEM((4, 2, 512, 256), F32),
            pltpu.VMEM((4, 2, 512, 128), BF16),
            pltpu.VMEM((2, 2, 256, 256), BF16),
            pltpu.VMEM((4, 2, 2, 256, 2, 128), F32),
            dma((8, 2)),
            dma((1,)),
        ],
        compiler_params=pltpu.CompilerParams(vmem_limit_bytes=VMEM_LIMIT),
    )(acc, exps, mcol, bt)
    return out.reshape(4, 512, 2, 256)


def solution(mesh):
    n = mesh.shape["region"]
    in_specs = (P("region", None, None, None), P("region", None)) + (P(),) * 8
    out_specs = P("region", None, None, None)
    return jax.shard_map(functools.partial(body, n), mesh=mesh, in_specs=in_specs, out_specs=out_specs, check_vma=False)
```

time: 54.2 us -> 37.7 us (0.70)
  Pallas kernels: 51.4 us -> 37.4 us
  local copies, waits for them, and re-layouts: 2.41 us -> 0 us
    pallas_call x3 -> x2, Pallas kernels: 51.4 us -> 37.4 us  [the longest x1 31.9 us: body(): pl.pallas_call(functools.partial(kernel_main, n), out_shape=(sds((4, 2, 5...]
    unnamed x1 -> x0, local copies, waits for them, and re-layouts: 2.41 us -> none
where the time goes in v1:
time: 37.7 us; the launch traced here: 37.6 us
  Pallas kernels  37.4 us (99%)
    pallas_call x1, Pallas kernels, body(): pl.pallas_call(functools.partial(kernel_main, n), out_shape=(sds((4, 2, 5...  31.9 us
    pallas_call x1, Pallas kernels, body(): pl.pallas_call(kernel_out, out_shape=sds((4, 256, 2, 2, 256), F32), in_sp...  5.46 us

profile of v1, /device:TPU:1, one launch (start us, length us, event | category | flops | bytes accessed | tf_op | source)
XLA Modules:
  0.0 37.6 jit_solution(13685743627664167821)
XLA Ops:
  0.0 31.9 %shard_map.100 = (f32[4,2,512,256]{3,2,1,0:T(8,128)}, bf16[2,512,256]{2,1,0:T(8,128)(2,1)}, bf16[4,2,512,128]{3,2,1,0:T(8,128)(2,1)}) custom-call(bf16[4,256,2,2,256]{4,3,2,1,0:T(2,128)(2,1)} %bitcast.8, bf16[2304,256]{1,0:T(8,128)(2,1)} %bitcast.9, f32[32,32,40]{2,1,0:T(8,128)} %bitcast.11, f32[32,32,160]{2,1,0:T(8,128)} %bitcast.10, s32[4,512]{1,0:T(4,128)} %valid.1, ...), custom_call_target="tpu_custom_call" | custom-call | tf_op jit(solution)/shard_map/pallas_call | solution.py:422
  31.9 5.5 %shard_map.101 = f32[4,256,2,2,256]{4,3,2,1,0:T(2,128)} custom-call(f32[4,2,512,256]{3,2,1,0:T(8,128)} %get-tuple-element.8.acc_any, bf16[2,512,256]{2,1,0:T(8,128)(2,1)} %get-tuple-element.9.exps, bf16[4,2,512,128]{3,2,1,0:T(8,128)(2,1)} %get-tuple-element.10.mcol_any, bf16[32,256]{1,0:T(8,128)(2,1)} %bitcast.13), custom_call_target="tpu_custom_call" | custom-call | tf_op jit(solution)/shard_map/pallas_call | solution.py:465

commit v2 on v1

--- a/solution.py
+++ b/solution.py
@@ -250,16 +250,16 @@
     for c in range(2):
         for m in range(512 // CHUNK):
             span = pl.ds(16 + m * CHUNK, CHUNK)
-            parts = [taps[i + a, ORDER[c][b], span] for a in rows for b in range(3)]
+            parts = [taps[i + a - 1, ORDER[c][b], span] for a in rows for b in range(3)]
             total = dot(jnp.concatenate(parts, 1), near[pl.ds(768 * first, 768 * count)])
             out = pl.ds(m * CHUNK, CHUNK)
             acc[i, c, out] = acc[i, c, out] + total if add else total
 
 
 def kernel_main(
-    n, x, near_any, coupling_any, top_any, valid, bt, transfer, partner_t, offset_t, count, acc_out, exp_out, mcol_out,
-    xs, near, coupling, top_c, mcol, taps, basis, packed, coef, coef_halo, hc, table, blocks, window, w_hi, w_lo, far,
-    acc, exps, v_ref, w_ref, path_ref, x_sem, w_sem, px_s, px_r, cf_s, cf_r, g_s, g_r, o_sem
+    n, x, near_any, coupling_any, top_any, valid, bt, transfer, partner_t, offset_t, count, acc, exps, mcol, hx,
+    xs, near, coupling, top_c, taps, basis, packed, inner_rows, outer, coef, coef_halo, hc, ho, table, blocks, window, w_hi, w_lo, far,
+    v_ref, w_ref, path_ref, x_sem, w_sem, px_s, px_r, cf_s, cf_r, g_s, g_r
 ):
     me = lax.axis_index("region")
     right, left = lax.rem(me + 1, n), lax.rem(me + n - 1, n)
@@ -277,8 +277,6 @@
         copy.start()
         return copy
 
-    for peer in [left, right] + peers1 + peers2:
-        pl.semaphore_signal(barrier, inc=1, device_id=(peer,), device_id_type=MESH)
     for i in (0, 3, 1, 2):
         for c in range(2):
             for lt in range(2):
@@ -286,6 +284,8 @@
     near_load = local(near_any, near, w_sem.at[0])
     coupling_load = local(coupling_any, coupling, w_sem.at[1])
     top_load = local(top_any, top_c, w_sem.at[2])
+    for peer in [left, right] + peers1 + peers2:
+        pl.semaphore_signal(barrier, inc=1, device_id=(peer,), device_id_type=MESH)
 
     basis[...] = jnp.zeros_like(basis)
     for at, i in enumerate(IN_ORDER):
@@ -300,9 +300,8 @@
             mcol[i, c] = col
             for lt in range(2):
                 part = xs.at[i, c, lt].reshape(512, 128)[...]
-                taps[i + 1, c, 16:528, lt * 128 : lt * 128 + 128] = part * col
-    mcol_copy = local(mcol, mcol_out, o_sem.at[0])
-    pixels = jnp.concatenate([taps[i + 1, c, 16:528] for i in range(4) for c in range(2)], 1)
+                taps[i, c, 16:528, lt * 128 : lt * 128 + 128] = part * col
+    pixels = jnp.concatenate([taps[i, c, 16:528] for i in range(4) for c in range(2)], 1)
     packed[...] = dot(pixels, basis[...], NT)
     top = climb(packed[...], v_ref, w_ref, paths)
     table[pl.ds(me, 1)] = jnp.concatenate([top[0:1], top[1:2], jnp.zeros((1, 64), F32)], 1).reshape(1, 1, 128)
@@ -311,68 +310,59 @@
     mine = table.at[pl.ds(me, 1)]
     for peer in peers1:
         remote(mine, mine, g_s.at[0], g_r.at[0], peer)
-    sent = packed.at[:, pl.ds(0, 128)]
+    for k in range(2):
+        row = packed[:, 128 + 64 * k : 192 + 64 * k]
+        outer[k] = jnp.concatenate([row[0:256], row[256:512]], 1)
+    inner_rows[...] = packed[:, 0:128]
     coef_copies = [
-        remote(sent, hc.at[0], cf_s.at[0], cf_r.at[0], right),
-        remote(sent, hc.at[1], cf_s.at[1], cf_r.at[1], left),
+        remote(inner_rows, hc.at[0], cf_s.at[0], cf_r.at[0], right),
+        remote(inner_rows, hc.at[1], cf_s.at[1], cf_r.at[1], left),
+        remote(outer.at[1], ho.at[0], cf_s.at[2], cf_r.at[2], right),
+        remote(outer.at[0], ho.at[1], cf_s.at[3], cf_r.at[3], left),
     ]
     inside = pl.ds(16, 512)
-    pixel_copies = [
-        remote(taps.at[4, pl.ds(0, 2), inside], taps.at[0, pl.ds(0, 2), inside], px_s.at[0], px_r.at[0], right),
-        remote(taps.at[1, pl.ds(0, 2), inside], taps.at[5, pl.ds(0, 2), inside], px_s.at[1], px_r.at[1], left),
-    ]
-
-    for r in range(1, 5):
+
+    for r in range(4):
         shifted(taps, r)
     near_load.wait()
     near_rows(taps, near, acc, 1, (0, 1, 2), False)
     near_rows(taps, near, acc, 2, (0, 1, 2), False)
+    near_rows(taps, near, acc, 0, (1, 2), False)
+    near_rows(taps, near, acc, 3, (0, 1), False)
+    coupling_load.wait()
+    far_weights(coupling, blocks, window, w_hi, w_lo)
+    coef[0:8] = jnp.zeros((8, 256), F32)
+    coef[520:528] = jnp.zeros((8, 256), F32)
+    coef[8:520] = packed[...]
+    far_field(coef, 0, w_hi, w_lo, far)
 
     await_bytes(table.at[pl.ds(0, 15)], g_s.at[0])
     await_bytes(table.at[pl.ds(0, 15)], g_r.at[0])
     block = table.at[pl.ds(group * 16, 16)]
     for peer in peers2:
         remote(block, block, g_s.at[1], g_r.at[1], peer)
-
-    inner_copy = local(acc.at[pl.ds(1, 2)], acc_out.at[pl.ds(1, 2)], o_sem.at[1])
-    coupling_load.wait()
-    far_weights(coupling, blocks, window, w_hi, w_lo)
+    pixel_copies = [
+        remote(taps.at[3, 0, inside], hx.at[0, 0], px_s.at[0], px_r.at[0], right),
+        remote(taps.at[0, 0, inside], hx.at[1, 0], px_s.at[1], px_r.at[1], left),
+    ]
+    pixel_copies += [
+        remote(taps.at[3, 1, inside], hx.at[0, 1], px_s.at[2], px_r.at[2], right),
+        remote(taps.at[0, 1, inside], hx.at[1, 1], px_s.at[3], px_r.at[3], left),
+    ]
+
     top_load.wait()
     slots = top_blocks(me, offset_t, top_c)
-    coef[0:8] = jnp.zeros((8, 256), F32)
-    coef[520:528] = jnp.zeros((8, 256), F32)
-    coef[8:520] = packed[...]
-    far_field(coef, 0, w_hi, w_lo, far)
-    near_rows(taps, near, acc, 0, (1, 2), False)
-    near_rows(taps, near, acc, 3, (0, 1), False)
-
-    for copy in pixel_copies:
-        copy.wait()
-
-    @pl.when(me == 0)
-    def _():
-        taps[0, 0:2, 16:528] = jnp.zeros((2, 512, 256), BF16)
-
-    @pl.when(me == n - 1)
-    def _():
-        taps[5, 0:2, 16:528] = jnp.zeros((2, 512, 256), BF16)
-
-    shifted(taps, 0)
-    shifted(taps, 5)
-    near_rows(taps, near, acc, 0, (0,), True)
-    near_rows(taps, near, acc, 3, (2,), True)
-    outer_copies = [local(acc.at[i], acc_out.at[i], o_sem.at[k]) for k, i in ((2, 0), (3, 3))]
 
     for copy in coef_copies:
         copy.wait()
     coef_halo[0:8] = jnp.zeros((8, 384), F32)
     coef_halo[520:528] = jnp.zeros((8, 384), F32)
-    coef_halo[8:520, 0:128] = hc[0] * jnp.where(me > 0, 1.0, 0.0)
-    coef_halo[8:520, 128:256] = hc[1] * jnp.where(me < n - 1, 1.0, 0.0)
-    for k, r in enumerate((0, 5)):
-        for c in range(2):
-            start = 256 + 64 * k + 32 * c
-            coef_halo[8:520, start : start + 32] = dot(taps[r, c, 16:528], bt[...], NT)
+    for k, inner in enumerate((jnp.where(me > 0, 1.0, 0.0), jnp.where(me < n - 1, 1.0, 0.0))):
+        coef_halo[8:520, 128 * k : 128 * k + 128] = hc[k] * inner
+        start = 256 + 64 * k
+        row = ho[k] * inner
+        coef_halo[8:264, start : start + 64] = row[:, 0:64]
+        coef_halo[264:520, start : start + 64] = row[:, 64:128]
     far_field(coef_halo, 1024, w_hi, w_lo, far)
 
     await_bytes(table.at[pl.ds(0, n - 16)], g_s.at[1])
@@ -383,28 +373,32 @@
     for half in range(2):
         exps[half, :, 0:128] = hi[:, half * 128 : half * 128 + 128]
         exps[half, :, 128:256] = lo[:, half * 128 : half * 128 + 128]
-    exp_copy = local(exps, exp_out, o_sem.at[4])
-    for copy in [mcol_copy, inner_copy] + outer_copies + [exp_copy]:
+    for copy in pixel_copies:
         copy.wait()
 
 
-def kernel_out(acc_any, exps, mcol_any, bt, out, acc, mcol, weight, os, in_sem, out_sem):
-    loads = [
-        (local(acc_any.at[i, c], acc.at[i, c], in_sem.at[i, c]), local(mcol_any.at[i, c], mcol.at[i, c], in_sem.at[4 + i, c]))
-        for i in range(4)
-        for c in range(2)
-    ]
+def kernel_out(n, acc, exps, mcol, hx, bt, near_any, out, weight, near, taps, os, in_sem, out_sem):
+    near_loads = [local(near_any.at[pl.ds(1536 * k, 768)], near.at[k], in_sem.at[k]) for k in range(2)]
+    me = lax.axis_index("region")
     weight[...] = jnp.zeros_like(weight)
     for i2 in range(2):
         for c in range(2):
             start = (1 - i2) * 64 + (1 - c) * 32
             weight[i2, c, pl.ds(start, 32)] = bt[...]
             weight[i2, c, pl.ds(128 + start, 32)] = bt[...]
-    for i in range(4):
+    for i in (1, 2, 0, 3):
+        edge = i // 3
+        if i in (0, 3):
+            inner = (jnp.where(me < n - 1, 1.0, 0.0) if edge else jnp.where(me > 0, 1.0, 0.0)).astype(BF16)
+            for c in range(2):
+                taps[edge, c, 16:528] = hx[edge, c] * inner
+            shifted(taps, edge)
+            near_loads[edge].wait()
         for c in range(2):
-            for copy in loads[i * 2 + c]:
-                copy.wait()
             total = acc[i, c] + dot(exps[1 - i // 2], weight[i % 2, c])
+            if i in (0, 3):
+                parts = [taps[edge, ORDER[c][b], 16:528] for b in range(3)]
+                total = total + dot(jnp.concatenate(parts, 1), near[edge])
             col = mcol[i, c].astype(F32)
             for lt in range(2):
                 os.at[i, c, lt].reshape(512, 128)[...] = total[:, lt * 128 : lt * 128 + 128] * col
@@ -415,68 +409,71 @@
 def body(n, pixels, valid, basis, near, transfer, coupling, top_c, partner, offset, count):
     x = pixels.reshape(4, 256, 2, 2, 256)
     bt = basis.T
+    near = near.reshape(2304, 256)
     vmem = pl.BlockSpec(memory_space=pltpu.VMEM)
     anywhere = pl.BlockSpec(memory_space=pl.ANY)
     sds = jax.ShapeDtypeStruct
     dma = pltpu.SemaphoreType.DMA
-    acc, exps, mcol = pl.pallas_call(
+    acc, exps, mcol, hx = pl.pallas_call(
         functools.partial(kernel_main, n),
-        out_shape=(sds((4, 2, 512, 256), F32), sds((2, 512, 256), BF16), sds((4, 2, 512, 128), BF16)),
+        out_shape=(
+            pltpu.VMEM((4, 2, 512, 256), F32), pltpu.VMEM((2, 512, 256), BF16), pltpu.VMEM((4, 2, 512, 128), BF16),
+            pltpu.VMEM((2, 2, 512, 256), BF16),
+        ),
         in_specs=[anywhere] * 4 + [vmem] * 5 + [pl.BlockSpec(memory_space=pltpu.SMEM)],
-        out_specs=(anywhere,) * 3,
+        out_specs=(vmem,) * 4,
         scratch_shapes=[
             pltpu.VMEM((4, 2, 2, 256, 2, 128), BF16),
             pltpu.VMEM((2304, 256), BF16),
             pltpu.VMEM((32, 32, 40), F32),
             pltpu.VMEM((32, 32, 160), F32),
-            pltpu.VMEM((4, 2, 512, 128), BF16),
-            pltpu.VMEM((6, 4, 544, 256), BF16),
+            pltpu.VMEM((4, 4, 544, 256), BF16),
             pltpu.VMEM((256, 2048), BF16),
             pltpu.VMEM((512, 256), F32),
+            pltpu.VMEM((512, 128), F32),
+            pltpu.VMEM((2, 256, 128), F32),
             pltpu.VMEM((528, 256), F32),
             pltpu.VMEM((528, 384), F32),
             pltpu.VMEM((2, 512, 128), F32),
+            pltpu.VMEM((2, 256, 128), F32),
             pltpu.VMEM((n, 1, 128), F32),
             pltpu.VMEM((1280, 128), F32),
             pltpu.VMEM((2, 8, 32, 1024), F32),
             pltpu.VMEM((2560, 256), BF16),
             pltpu.VMEM((2560, 256), BF16),
             pltpu.VMEM((512, 256), F32),
-            pltpu.VMEM((4, 2, 512, 256), F32),
-            pltpu.VMEM((2, 512, 256), BF16),
             pltpu.VMEM((512, 128), F32),
             pltpu.VMEM((32, 128), F32),
             pltpu.VMEM((448, 128), F32),
             dma((4,)),
             dma((3,)),
+            dma((4,)),
+            dma((4,)),
+            dma((4,)),
+            dma((4,)),
             dma((2,)),
             dma((2,)),
-            dma((2,)),
-            dma((2,)),
-            dma((2,)),
-            dma((2,)),
-            dma((5,)),
         ],
         compiler_params=pltpu.CompilerParams(collective_id=0, has_side_effects=True, vmem_limit_bytes=VMEM_LIMIT),
     )(
-        x, near.reshape(2304, 256), jnp.transpose(coupling, (1, 2, 0)), jnp.transpose(top_c, (1, 2, 0)),
+        x, near, jnp.transpose(coupling, (1, 2, 0)), jnp.transpose(top_c, (1, 2, 0)),
         valid, bt, transfer, partner.T, offset.T, count,
     )
     out = pl.pallas_call(
-        kernel_out,
+        functools.partial(kernel_out, n),
         out_shape=sds((4, 256, 2, 2, 256), F32),
-        in_specs=[anywhere, vmem, anywhere, vmem],
+        in_specs=[vmem] * 5 + [anywhere],
         out_specs=anywhere,
         scratch_shapes=[
-            pltpu.VMEM((4, 2, 512, 256), F32),
-            pltpu.VMEM((4, 2, 512, 128), BF16),
             pltpu.VMEM((2, 2, 256, 256), BF16),
+            pltpu.VMEM((2, 768, 256), BF16),
+            pltpu.VMEM((2, 4, 544, 256), BF16),
             pltpu.VMEM((4, 2, 2, 256, 2, 128), F32),
-            dma((8, 2)),
+            dma((2,)),
             dma((1,)),
         ],
-        compiler_params=pltpu.CompilerParams(vmem_limit_bytes=VMEM_LIMIT),
-    )(acc, exps, mcol, bt)
+        compiler_params=pltpu.CompilerParams(vmem_limit_bytes=24 << 20),
+    )(*(pltpu.with_memory_space_constraint(a, pltpu.VMEM) for a in (acc, exps, mcol, hx)), bt, near)
     return out.reshape(4, 512, 2, 256)
 
 

time: 37.7 us -> 32.2 us (0.85)
  the two profiles are of different devices: /device:TPU:1 before, /device:TPU:0 now
where the time goes in v2:
time: 32.2 us; the launch traced here: 31.9 us
  Pallas kernels  31.9 us (99%)
    pallas_call x1, Pallas kernels, body(): pl.pallas_call(functools.partial(kernel_main, n), out_shape=(pltpu.VMEM((...  28.4 us
    pallas_call x1, Pallas kernels, body(): pl.pallas_call(functools.partial(kernel_out, n), out_shape=sds((4, 256, 2...  3.53 us

profile of v2, /device:TPU:0, one launch (start us, length us, event | category | flops | bytes accessed | tf_op | source)
XLA Modules:
  0.0 31.9 jit_solution(6461158083195087000)
XLA Ops:
  0.0 0.0 copy-start
  0.0 0.0 copy-start.1
  0.0 28.4 %shard_map.100 = (f32[4,2,512,256]{3,2,1,0:T(8,128)S(1)}, bf16[2,512,256]{2,1,0:T(8,128)(2,1)S(1)}, bf16[4,2,512,128]{3,2,1,0:T(8,128)(2,1)S(1)}, bf16[2,2,512,256]{3,2,1,0:T(8,128)(2,1)S(1)}) custom-call(bf16[4,256,2,2,256]{4,3,2,1,0:T(2,128)(2,1)} %bitcast.12, bf16[2304,256]{1,0:T(8,128)(2,1)} %bitcast.8, f32[32,32,40]{2,1,0:T(8,128)} %bitcast.14, ...), custom_call_target="tpu_custom_call" | custom-call | tf_op jit(solution)/shard_map/pallas_call | solution.py:417
  28.4 0.0 copy-done
  28.4 0.0 copy-done.1
  28.4 3.5 %shard_map.101 = f32[4,256,2,2,256]{4,3,2,1,0:T(2,128)} custom-call(f32[4,2,512,256]{3,2,1,0:T(8,128)S(1)} %get-tuple-element.9.acc, bf16[2,512,256]{2,1,0:T(8,128)(2,1)S(1)} %get-tuple-element.10.exps, bf16[4,2,512,128]{3,2,1,0:T(8,128)(2,1)S(1)} %get-tuple-element.11.mcol, bf16[2,2,512,256]{3,2,1,0:T(8,128)(2,1)S(1)} %get-tuple-element.12.hx, ...), custom_call_target="tpu_custom_call" | custom-call | tf_op jit(solution)/shard_map/pallas_call | solution.py:462
Async XLA Ops:
  0.0 28.4 %copy-start = (bf16[9,256,256]{2,1,0:T(8,128)(2,1)S(1)}, bf16[9,256,256]{2,1,0:T(8,128)(2,1)}, u32[]{:S(2)}) copy-start(bf16[9,256,256]{2,1,0:T(8,128)(2,1)} %param.13) | copy-start | bytes 3538948
  0.0 28.4 %copy-start.1 = (bf16[256,32]{0,1:T(8,128)(2,1)S(1)}, bf16[256,32]{0,1:T(8,128)(2,1)}, u32[]{:S(2)}) copy-start(bf16[256,32]{0,1:T(8,128)(2,1)} %param.12) | copy-start | bytes 49156

commit v3 on v2

--- a/solution.py
+++ b/solution.py
@@ -29,6 +29,11 @@
     a_hi, a_lo = split(a)
     b_hi, b_lo = split(b)
     return dot(a_hi, b_hi, dims) + (dot(a_lo, b_hi, dims) + dot(a_hi, b_lo, dims))
+
+
+def dot3_ready(a, b, dims=NN):
+    a_hi, a_lo = split(a)
+    return dot(a_hi, b[0], dims) + (dot(a_lo, b[0], dims) + dot(a_hi, b[1], dims))
 
 
 def iota(shape, axis):
@@ -74,12 +79,14 @@
     )
 
 
-def climb(packed, v_ref, w_ref, paths):
-    _, _, three, four = paths
-    merge = jnp.concatenate(
-        [three[(c * 4 + i) * 32 : (c * 4 + i) * 32 + 32] for i in IN_ORDER for c in range(2)], 0
+def leaf_paths(three, rows, sides):
+    return jnp.concatenate(
+        [three[(c * 4 + i) * 32 : (c * 4 + i) * 32 + 32] for i in rows for c in sides], 0
     )
-    v_ref[:, 0:32] = dot3(packed, merge)
+
+
+def climb(packed, v_ref, w_ref, merge, four):
+    v_ref[:, 0:32] = dot3_ready(packed, merge)
     rows = []
     for rhs in range(2):
         rows.append(
@@ -87,9 +94,9 @@
                 [v_ref[pl.ds(2 * b + rhs, 16, stride=32), :][:, 0:32] for b in range(16)], 1
             )
         )
-    w_ref[:, 0:32] = dot3(jnp.concatenate(rows, 0), four)
+    w_ref[:, 0:32] = dot3_ready(jnp.concatenate(rows, 0), four)
     last = jnp.concatenate([w_ref[pl.ds(a, 2, stride=16), :][:, 0:32] for a in range(16)], 1)
-    return dot3(jnp.concatenate([last, last, last, last], 0), four)[0:2]
+    return dot3_ready(jnp.concatenate([last, last, last, last], 0), four)[0:2]
 
 
 def top_blocks(me, offset_t, top_c):
@@ -105,8 +112,7 @@
     return dot(hi, pick, NT) + dot(lo, pick, NT)
 
 
-def top_expand(me, table, partner_t, count, blocks, paths, path_ref):
-    both, two, three, _ = paths
+def top_picks(me, partner_t, count):
     bases = (0, 256, 384, 448)
     lane = iota((8, 480), 1)
     slot = iota((8, 256), 0)
@@ -119,10 +125,25 @@
         live = slot < count[row]
         for t in range(2**h):
             picks.append(jnp.where(live & (node == chosen * 2**h + t), 1.0, 0.0))
-    pick = jnp.concatenate(picks, 0).astype(BF16)
+    return jnp.concatenate(picks, 0).astype(BF16)
+
+
+def root_paths(me, paths, path_ref):
+    both, two, three, four = paths
+    path_ref[0:64, 0:32] = both
+    path_ref[64:192, 0:32] = two
+    path_ref[192:448, 0:32] = three
+    starts = (0, 0, 64, 192)
+    parts = [four]
+    for h in range(1, 4):
+        begin = pl.multiple_of(starts[h] + (me & (2**h - 1)) * 32, 32)
+        parts.append(dot3(four, path_ref[pl.ds(begin, 32), :][:, 0:32]))
+    return jnp.concatenate(parts, 1)
+
+
+def top_expand(table, pick, blocks, stacks):
     hi, lo = split(table)
     picked = dot(pick, hi) + dot(pick, lo)
-    stacks = (None, both, two, three)
     first = 0
     nodes = [[], []]
     for h in range(4):
@@ -139,7 +160,7 @@
             )
         merged = jnp.concatenate(merged, 0)
         if h > 0:
-            merged = dot3(merged, stacks[h])
+            merged = dot3_ready(merged, stacks[h])
         nodes[0].append(merged[0:8])
         nodes[1].append(merged[8:16])
         first += 8 * 2**h
@@ -150,40 +171,21 @@
         for a in range(32):
             total = total + blocks[32 * a : 32 * a + 32] * across[a : a + 1]
         total = total.T
-        local.append([jnp.sum(total[8 * h : 8 * h + 8], 0, keepdims=True) for h in range(4)])
-    path_ref[0:64, 0:32] = both
-    path_ref[64:192, 0:32] = two
-    path_ref[192:448, 0:32] = three
-    expansion = jnp.concatenate([local[0][0], local[1][0]] * 4, 0)
-    starts = (0, 0, 64, 192)
-    for h in range(1, 4):
-        here = jnp.concatenate([local[0][h], local[1][h]] * 4, 0)
-        begin = pl.multiple_of(starts[h] + (me & (2**h - 1)) * 32, 32)
-        path = path_ref[pl.ds(begin, 32), :][:, 0:32]
-        expansion = expansion + dot3(here, path, NT)
-    return expansion[0:2]
-
-
-def descend(expansion, v_ref, w_ref, paths):
-    _, _, three, four = paths
-    wide = dot3(jnp.concatenate([expansion] * 4, 0), four, NT)[0:2]
+        local.append(jnp.concatenate([jnp.sum(total[8 * h : 8 * h + 8], 0, keepdims=True) for h in range(4)], 1))
+    return jnp.concatenate(local * 4, 0)
+
+
+def descend(local, v_ref, w_ref, roots, four, merge):
+    wide = dot3_ready(local, roots, NT)[0:2]
     for a in range(16):
         w_ref[pl.ds(a, 2, stride=16), 0:32] = wide[:, 32 * a : 32 * a + 32]
-    wide = dot3(w_ref[:, 0:32], four, NT)
+    wide = dot3_ready(w_ref[:, 0:32], four, NT)
     for rhs in range(2):
         for b in range(16):
             v_ref[pl.ds(2 * b + rhs, 16, stride=32), 0:32] = wide[
                 16 * rhs : 16 * rhs + 16, 32 * b : 32 * b + 32
             ]
-    merge = jnp.concatenate(
-        [
-            three[(c * 4 + i) * 32 : (c * 4 + i) * 32 + 32]
-            for i in (3, 2, 1, 0)
-            for c in (1, 0)
-        ],
-        0,
-    )
-    return dot3(v_ref[:, 0:32], merge, NT)
+    return dot3_ready(v_ref[:, 0:32], merge, NT)
 
 
 OFFSETS = [(a, b) for a in range(-3, 4) for b in range(-3, 4) if max(abs(a), abs(b)) >= 2]
@@ -257,23 +259,28 @@
 
 
 def kernel_main(
-    n, x, near_any, coupling_any, top_any, valid, bt, transfer, partner_t, offset_t, count, acc, exps, mcol, hx,
-    xs, near, coupling, top_c, taps, basis, packed, inner_rows, outer, coef, coef_halo, hc, ho, table, blocks, window, w_hi, w_lo, far,
+    n, x, near_any, coupling_any, top_any, valid, bt, transfer, partner_t, offset_t, count, acc, exps, mcol, hx, weight, near_out,
+    xs, near, coupling, top_c, taps, edge_taps, basis, packed, inner_rows, outer, coef, coef_halo, hc, ho, table, blocks, window, w_hi, w_lo, far,
     v_ref, w_ref, path_ref, x_sem, w_sem, px_s, px_r, cf_s, cf_r, g_s, g_r
 ):
     me = lax.axis_index("region")
     right, left = lax.rem(me + 1, n), lax.rem(me + n - 1, n)
     group = me // 16
     spot = lax.rem(me, 16)
+    core = lax.rem(me, 2)
+    edge = 1 - core
     groups = n // 16
     barrier = pltpu.get_barrier_semaphore()
     peers1 = [group * 16 + lax.rem(spot + k, 16) for k in range(1, 16)]
     peers2 = [lax.rem(group + k, groups) * 16 + spot for k in range(1, groups)]
 
-    def remote(src, dst, send, recv, peer):
-        copy = pltpu.make_async_remote_copy(
+    def remote_copy(src, dst, send, recv, peer):
+        return pltpu.make_async_remote_copy(
             src_ref=src, dst_ref=dst, send_sem=send, recv_sem=recv, device_id=(peer,), device_id_type=MESH
         )
+
+    def remote(*args):
+        copy = remote_copy(*args)
         copy.start()
         return copy
 
@@ -292,6 +299,8 @@
         for c in range(2):
             basis[pl.ds(at * 64 + c * 32, 32), pl.ds((i * 2 + c) * 256, 256)] = bt[...]
     paths = tree_paths(transfer)
+    four = split(paths[3])
+    merge_up = split(leaf_paths(paths[2], IN_ORDER, (0, 1)))
     rows = mask_rows(valid[...])
     for i in (0, 3, 1, 2):
         await_bytes(xs.at[i], x_sem.at[i])
@@ -303,7 +312,7 @@
                 taps[i, c, 16:528, lt * 128 : lt * 128 + 128] = part * col
     pixels = jnp.concatenate([taps[i, c, 16:528] for i in range(4) for c in range(2)], 1)
     packed[...] = dot(pixels, basis[...], NT)
-    top = climb(packed[...], v_ref, w_ref, paths)
+    top = climb(packed[...], v_ref, w_ref, merge_up, four)
     table[pl.ds(me, 1)] = jnp.concatenate([top[0:1], top[1:2], jnp.zeros((1, 64), F32)], 1).reshape(1, 1, 128)
 
     pl.semaphore_wait(barrier, 2 + 15 + groups - 1)
@@ -321,10 +330,27 @@
         remote(outer.at[0], ho.at[1], cf_s.at[3], cf_r.at[3], left),
     ]
     inside = pl.ds(16, 512)
-
+    to_right = remote_copy(taps.at[3, pl.ds(0, 2), inside], hx.at[0], px_s.at[0], px_r.at[0], right)
+    to_left = remote_copy(taps.at[0, pl.ds(0, 2), inside], hx.at[1], px_s.at[1], px_r.at[1], left)
+
+    @pl.when(core == 0)
+    def _():
+        to_right.start()
+
+    @pl.when(core == 1)
+    def _():
+        to_left.start()
+
+    weight[...] = jnp.zeros_like(weight)
+    for i2 in range(2):
+        for c in range(2):
+            start = (1 - i2) * 64 + (1 - c) * 32
+            weight[i2, c, pl.ds(start, 32)] = bt[...]
+            weight[i2, c, pl.ds(128 + start, 32)] = bt[...]
     for r in range(4):
         shifted(taps, r)
     near_load.wait()
+    near_out[...] = near[pl.ds(pl.multiple_of(1536 * core, 256), 768)]
     near_rows(taps, near, acc, 1, (0, 1, 2), False)
     near_rows(taps, near, acc, 2, (0, 1, 2), False)
     near_rows(taps, near, acc, 0, (1, 2), False)
@@ -336,22 +362,36 @@
     coef[8:520] = packed[...]
     far_field(coef, 0, w_hi, w_lo, far)
 
-    await_bytes(table.at[pl.ds(0, 15)], g_s.at[0])
     await_bytes(table.at[pl.ds(0, 15)], g_r.at[0])
     block = table.at[pl.ds(group * 16, 16)]
     for peer in peers2:
         remote(block, block, g_s.at[1], g_r.at[1], peer)
-    pixel_copies = [
-        remote(taps.at[3, 0, inside], hx.at[0, 0], px_s.at[0], px_r.at[0], right),
-        remote(taps.at[0, 0, inside], hx.at[1, 0], px_s.at[1], px_r.at[1], left),
-    ]
-    pixel_copies += [
-        remote(taps.at[3, 1, inside], hx.at[0, 1], px_s.at[2], px_r.at[2], right),
-        remote(taps.at[0, 1, inside], hx.at[1, 1], px_s.at[3], px_r.at[3], left),
-    ]
+
+    @pl.when(core == 1)
+    def _():
+        to_right.start()
+
+    @pl.when(core == 0)
+    def _():
+        to_left.start()
 
     top_load.wait()
     slots = top_blocks(me, offset_t, top_c)
+    pick = top_picks(me, partner_t, count)
+    stacks = (None,) + tuple(split(path) for path in paths[:3])
+    roots = split(root_paths(me, paths, path_ref))
+    merge_down = split(leaf_paths(paths[2], (3, 2, 1, 0), (1, 0)))
+
+    await_bytes(hx.at[0], px_r.at[edge])
+    edge_taps[0, 0, inside] = hx[edge, 0]
+    edge_taps[0, 1, inside] = hx[edge, 1]
+    shifted(edge_taps, 0)
+    for c in range(2):
+        for m in range(512 // CHUNK):
+            parts = [edge_taps[0, ORDER[c][b], pl.ds(16 + m * CHUNK, CHUNK)] for b in range(3)]
+            rows = pl.ds(m * CHUNK, CHUNK)
+            begin = pl.multiple_of(1536 * edge, 256)
+            acc[3 * edge, c, rows] += dot(jnp.concatenate(parts, 1), near[pl.ds(begin, 768)])
 
     for copy in coef_copies:
         copy.wait()
@@ -365,44 +405,39 @@
         coef_halo[264:520, start : start + 64] = row[:, 64:128]
     far_field(coef_halo, 1024, w_hi, w_lo, far)
 
-    await_bytes(table.at[pl.ds(0, n - 16)], g_s.at[1])
     await_bytes(table.at[pl.ds(0, n - 16)], g_r.at[1])
-    expansion = top_expand(me, table.reshape(n, 128)[...], partner_t, count, slots, paths, path_ref)
-    leaf = descend(expansion, v_ref, w_ref, paths) + far[...]
+    local_exp = top_expand(table.reshape(n, 128)[...], pick, slots, stacks)
+    leaf = descend(local_exp, v_ref, w_ref, roots, four, merge_down) + far[...]
     hi, lo = split(leaf)
     for half in range(2):
         exps[half, :, 0:128] = hi[:, half * 128 : half * 128 + 128]
         exps[half, :, 128:256] = lo[:, half * 128 : half * 128 + 128]
-    for copy in pixel_copies:
-        copy.wait()
-
-
-def kernel_out(n, acc, exps, mcol, hx, bt, near_any, out, weight, near, taps, os, in_sem, out_sem):
-    near_loads = [local(near_any.at[pl.ds(1536 * k, 768)], near.at[k], in_sem.at[k]) for k in range(2)]
+    await_bytes(hx.at[0], px_r.at[core])
+    await_bytes(hx.at[0], px_s.at[0])
+    await_bytes(hx.at[0], px_s.at[1])
+    await_bytes(table.at[pl.ds(0, 15)], g_s.at[0])
+    await_bytes(table.at[pl.ds(0, n - 16)], g_s.at[1])
+
+
+def kernel_out(n, acc, exps, mcol, hx, weight, near, out, taps, os, out_sem):
     me = lax.axis_index("region")
-    weight[...] = jnp.zeros_like(weight)
-    for i2 in range(2):
+    edge = lax.rem(me, 2)
+    for at, (i, side) in enumerate(((1, 1), (2, 0), (3 - 3 * edge, 1 - edge), (3 * edge, edge))):
+        half = 1 - side if at >= 2 else 1 - i // 2
+        if at == 3:
+            inner = jnp.where(edge == 0, me > 0, me < n - 1).astype(F32).astype(BF16)
+            for c in range(2):
+                taps[0, c, 16:528] = hx[edge, c] * inner
+            shifted(taps, 0)
         for c in range(2):
-            start = (1 - i2) * 64 + (1 - c) * 32
-            weight[i2, c, pl.ds(start, 32)] = bt[...]
-            weight[i2, c, pl.ds(128 + start, 32)] = bt[...]
-    for i in (1, 2, 0, 3):
-        edge = i // 3
-        if i in (0, 3):
-            inner = (jnp.where(me < n - 1, 1.0, 0.0) if edge else jnp.where(me > 0, 1.0, 0.0)).astype(BF16)
-            for c in range(2):
-                taps[edge, c, 16:528] = hx[edge, c] * inner
-            shifted(taps, edge)
-            near_loads[edge].wait()
-        for c in range(2):
-            total = acc[i, c] + dot(exps[1 - i // 2], weight[i % 2, c])
-            if i in (0, 3):
-                parts = [taps[edge, ORDER[c][b], 16:528] for b in range(3)]
-                total = total + dot(jnp.concatenate(parts, 1), near[edge])
+            total = acc[i, c] + dot(exps[half], weight[side, c])
+            if at == 3:
+                parts = [taps[0, ORDER[c][b], 16:528] for b in range(3)]
+                total = total + dot(jnp.concatenate(parts, 1), near[...])
             col = mcol[i, c].astype(F32)
             for lt in range(2):
-                os.at[i, c, lt].reshape(512, 128)[...] = total[:, lt * 128 : lt * 128 + 128] * col
-                local(os.at[i, c, lt], out.at[i, :, c, :, pl.ds(lt * 128, 128)], out_sem.at[0])
+                os.at[at, c, lt].reshape(512, 128)[...] = total[:, lt * 128 : lt * 128 + 128] * col
+                local(os.at[at, c, lt], out.at[i, :, c, :, pl.ds(lt * 128, 128)], out_sem.at[0])
     await_bytes(os, out_sem.at[0])
 
 
@@ -414,20 +449,23 @@
     anywhere = pl.BlockSpec(memory_space=pl.ANY)
     sds = jax.ShapeDtypeStruct
     dma = pltpu.SemaphoreType.DMA
-    acc, exps, mcol, hx = pl.pallas_call(
+    passed = pl.pallas_call(
         functools.partial(kernel_main, n),
         out_shape=(
             pltpu.VMEM((4, 2, 512, 256), F32), pltpu.VMEM((2, 512, 256), BF16), pltpu.VMEM((4, 2, 512, 128), BF16),
             pltpu.VMEM((2, 2, 512, 256), BF16),
+            pltpu.VMEM((2, 2, 256, 256), BF16),
+            pltpu.VMEM((768, 256), BF16),
         ),
         in_specs=[anywhere] * 4 + [vmem] * 5 + [pl.BlockSpec(memory_space=pltpu.SMEM)],
-        out_specs=(vmem,) * 4,
+        out_specs=(vmem,) * 6,
         scratch_shapes=[
             pltpu.VMEM((4, 2, 2, 256, 2, 128), BF16),
             pltpu.VMEM((2304, 256), BF16),
             pltpu.VMEM((32, 32, 40), F32),
             pltpu.VMEM((32, 32, 160), F32),
             pltpu.VMEM((4, 4, 544, 256), BF16),
+            pltpu.VMEM((1, 4, 544, 256), BF16),
             pltpu.VMEM((256, 2048), BF16),
             pltpu.VMEM((512, 256), F32),
             pltpu.VMEM((512, 128), F32),
@@ -462,18 +500,15 @@
     out = pl.pallas_call(
         functools.partial(kernel_out, n),
         out_shape=sds((4, 256, 2, 2, 256), F32),
-        in_specs=[vmem] * 5 + [anywhere],
+        in_specs=[vmem] * 6,
         out_specs=anywhere,
         scratch_shapes=[
-            pltpu.VMEM((2, 2, 256, 256), BF16),
-            pltpu.VMEM((2, 768, 256), BF16),
-            pltpu.VMEM((2, 4, 544, 256), BF16),
+            pltpu.VMEM((1, 4, 544, 256), BF16),
             pltpu.VMEM((4, 2, 2, 256, 2, 128), F32),
-            dma((2,)),
             dma((1,)),
         ],
         compiler_params=pltpu.CompilerParams(vmem_limit_bytes=24 << 20),
-    )(*(pltpu.with_memory_space_constraint(a, pltpu.VMEM) for a in (acc, exps, mcol, hx)), bt, near)
+    )(*(pltpu.with_memory_space_constraint(a, pltpu.VMEM) for a in passed))
     return out.reshape(4, 512, 2, 256)
 
 

time: 32.2 us -> 31.2 us (0.969)
  Pallas kernels: 31.9 us -> 30.9 us
    pallas_call x1, Pallas kernels: 3.53 us -> 2.41 us  [body(): pl.pallas_call(functools.partial(kernel_out, n), out_shape=sds((4, 256, 2...]
where the time goes in v3:
time: 31.2 us; the launch traced here: 31 us
  Pallas kernels  30.9 us (99%)
    pallas_call x1, Pallas kernels, body(): pl.pallas_call(functools.partial(kernel_main, n), out_shape=(pltpu.VMEM((...  28.4 us
    pallas_call x1, Pallas kernels, body(): pl.pallas_call(functools.partial(kernel_out, n), out_shape=sds((4, 256, 2...  2.41 us

profile of v3, /device:TPU:0, one launch (start us, length us, event | category | flops | bytes accessed | tf_op | source)
XLA Modules:
  0.0 31.0 jit_solution(12703737403776456082)
XLA Ops:
  0.0 28.4 %shard_map.100 = (f32[4,2,512,256]{3,2,1,0:T(8,128)S(1)}, bf16[2,512,256]{2,1,0:T(8,128)(2,1)S(1)}, bf16[4,2,512,128]{3,2,1,0:T(8,128)(2,1)S(1)}, bf16[2,2,512,2...) custom-call(bf16[4,256,2,2,256]{4,3,2,1,0:T(2,128)(2,1)} %bitcast.8, ...), custom_call_target="tpu_custom_call" | custom-call | tf_op jit(solution)/shard_map/pallas_call | solution.py:452
  28.5 2.4 %shard_map.101 = f32[4,256,2,2,256]{4,3,2,1,0:T(2,128)} custom-call(f32[4,2,512,256]{3,2,1,0:T(8,128)S(1)} %get-tuple-element.11.acc, bf16[2,512,256]{2,1,0:T(8,128)(2,1)S(1)} %get-tuple-element.12.exps, bf16[4,2,512,128]{3,2,1,0:T(8,128)(2,1)S(1)} %get-tuple-element.13.mcol, bf16[2,2,512,256]{3,2,1,0:T(8,128)(2,1)S(1)} %get-tuple-element.14.hx, ...), custom_call_target="tpu_custom_call" | custom-call | tf_op jit(solution)/shard_map/pallas_call | solution.py:500

commit v4 on v3

--- a/solution.py
+++ b/solution.py
@@ -357,24 +357,24 @@
     near_rows(taps, near, acc, 3, (0, 1), False)
     coupling_load.wait()
     far_weights(coupling, blocks, window, w_hi, w_lo)
+
+    await_bytes(table.at[pl.ds(0, 15)], g_r.at[0])
+    block = table.at[pl.ds(group * 16, 16)]
+    for peer in peers2:
+        remote(block, block, g_s.at[1], g_r.at[1], peer)
+
+    @pl.when(core == 1)
+    def _():
+        to_right.start()
+
+    @pl.when(core == 0)
+    def _():
+        to_left.start()
+
     coef[0:8] = jnp.zeros((8, 256), F32)
     coef[520:528] = jnp.zeros((8, 256), F32)
     coef[8:520] = packed[...]
     far_field(coef, 0, w_hi, w_lo, far)
-
-    await_bytes(table.at[pl.ds(0, 15)], g_r.at[0])
-    block = table.at[pl.ds(group * 16, 16)]
-    for peer in peers2:
-        remote(block, block, g_s.at[1], g_r.at[1], peer)
-
-    @pl.when(core == 1)
-    def _():
-        to_right.start()
-
-    @pl.when(core == 0)
-    def _():
-        to_left.start()
-
     top_load.wait()
     slots = top_blocks(me, offset_t, top_c)
     pick = top_picks(me, partner_t, count)

time: 31.2 us -> 30.3 us (0.971)
  Pallas kernels: 30.9 us -> 30 us
    pallas_call x1, Pallas kernels: 28.4 us -> 27.6 us  [body(): pl.pallas_call(functools.partial(kernel_main, n), out_shape=(pltpu.VMEM((...]
where the time goes in v4:
time: 30.3 us; the launch traced here: 30.2 us
  Pallas kernels  30 us (99%)
    pallas_call x1, Pallas kernels, body(): pl.pallas_call(functools.partial(kernel_main, n), out_shape=(pltpu.VMEM((...  27.6 us
    pallas_call x1, Pallas kernels, body(): pl.pallas_call(functools.partial(kernel_out, n), out_shape=sds((4, 256, 2...  2.41 us

profile of v4, /device:TPU:0, one launch (start us, length us, event | category | flops | bytes accessed | tf_op | source)
XLA Modules:
  0.0 30.2 jit_solution(11169141496258137849)
XLA Ops:
  0.0 27.6 %shard_map.100 = (f32[4,2,512,256]{3,2,1,0:T(8,128)S(1)}, bf16[2,512,256]{2,1,0:T(8,128)(2,1)S(1)}, bf16[4,2,512,128]{3,2,1,0:T(8,128)(2,1)S(1)}, bf16[2,2,512,2...) custom-call(bf16[4,256,2,2,256]{4,3,2,1,0:T(2,128)(2,1)} %bitcast.8, ...), custom_call_target="tpu_custom_call" | custom-call | tf_op jit(solution)/shard_map/pallas_call | solution.py:452
  27.6 2.4 %shard_map.101 = f32[4,256,2,2,256]{4,3,2,1,0:T(2,128)} custom-call(f32[4,2,512,256]{3,2,1,0:T(8,128)S(1)} %get-tuple-element.11.acc, bf16[2,512,256]{2,1,0:T(8,128)(2,1)S(1)} %get-tuple-element.12.exps, bf16[4,2,512,128]{3,2,1,0:T(8,128)(2,1)S(1)} %get-tuple-element.13.mcol, bf16[2,2,512,256]{3,2,1,0:T(8,128)(2,1)S(1)} %get-tuple-element.14.hx, ...), custom_call_target="tpu_custom_call" | custom-call | tf_op jit(solution)/shard_map/pallas_call | solution.py:500

commit v5 on v4

--- a/solution.py
+++ b/solution.py
@@ -288,11 +288,11 @@
         for c in range(2):
             for lt in range(2):
                 local(x.at[i, :, c, :, pl.ds(lt * 128, 128)], xs.at[i, c, lt], x_sem.at[i])
+    for peer in [left, right] + peers1 + peers2:
+        pl.semaphore_signal(barrier, inc=1, device_id=(peer,), device_id_type=MESH)
     near_load = local(near_any, near, w_sem.at[0])
     coupling_load = local(coupling_any, coupling, w_sem.at[1])
     top_load = local(top_any, top_c, w_sem.at[2])
-    for peer in [left, right] + peers1 + peers2:
-        pl.semaphore_signal(barrier, inc=1, device_id=(peer,), device_id_type=MESH)
 
     basis[...] = jnp.zeros_like(basis)
     for at, i in enumerate(IN_ORDER):

time: 30.3 us -> 30.3 us (level)
  no operation moved by 1% of the time
where the time goes in v5:
time: 30.3 us; the launch traced here: 30.2 us
  Pallas kernels  30 us (99%)
    pallas_call x1, Pallas kernels, body(): pl.pallas_call(functools.partial(kernel_main, n), out_shape=(pltpu.VMEM((...  27.6 us
    pallas_call x1, Pallas kernels, body(): pl.pallas_call(functools.partial(kernel_out, n), out_shape=sds((4, 256, 2...  2.41 us

profile of v5, /device:TPU:0, one launch (start us, length us, event | category | flops | bytes accessed | tf_op | source)
XLA Modules:
  0.0 30.2 jit_solution(7004997292222554154)
XLA Ops:
  0.0 27.6 %shard_map.100 = (f32[4,2,512,256]{3,2,1,0:T(8,128)S(1)}, bf16[2,512,256]{2,1,0:T(8,128)(2,1)S(1)}, bf16[4,2,512,128]{3,2,1,0:T(8,128)(2,1)S(1)}, bf16[2,2,512,2...) custom-call(bf16[4,256,2,2,256]{4,3,2,1,0:T(2,128)(2,1)} %bitcast.8, ...), custom_call_target="tpu_custom_call" | custom-call | tf_op jit(solution)/shard_map/pallas_call | solution.py:452
  27.6 2.4 %shard_map.101 = f32[4,256,2,2,256]{4,3,2,1,0:T(2,128)} custom-call(f32[4,2,512,256]{3,2,1,0:T(8,128)S(1)} %get-tuple-element.11.acc, bf16[2,512,256]{2,1,0:T(8,128)(2,1)S(1)} %get-tuple-element.12.exps, bf16[4,2,512,128]{3,2,1,0:T(8,128)(2,1)S(1)} %get-tuple-element.13.mcol, bf16[2,2,512,256]{3,2,1,0:T(8,128)(2,1)S(1)} %get-tuple-element.14.hx, ...), custom_call_target="tpu_custom_call" | custom-call | tf_op jit(solution)/shard_map/pallas_call | solution.py:500
